TPU v7x, 512 devices: a whole 4x4x16 slice. The times are simulated.
512 devices in a mesh: blk: 64 (over z_lo, x, core), col: 8 (over y, z_hi).
Axes of the slice: x: 4, y: 4, z: 16 (z_hi: 2, z_lo: 8; z = z_hi * 8 + z_lo), core: 2. Of those that a mesh axis runs over, the one named last changes fastest.
Arguments:
- word_vectors: float32 [300, 131072], P(None, ('blk', 'col')), may hold values from -0.6 to 0.6
- word_bias: float32 [131072], P(('blk', 'col')), may hold values from -3 to 3
- context_vectors: float32 [300, 131072], P(None, ('blk', 'col')), may hold values from -0.6 to 0.6
- context_bias: float32 [131072], P(('blk', 'col')), may hold values from -3 to 3
- counts: bfloat16 [2, 131072, 2048], P(None, 'blk', 'col'), may hold values from 0.25 to 400
- tile_mask: int32 [2, 1024, 16], P(None, 'blk', 'col'), may hold values 0 or 1
Outputs:
- new_word_vectors: float32 [300, 131072], P(None, ('blk', 'col'))
- new_word_bias: float32 [131072], P(('blk', 'col'))
- new_context_vectors: float32 [300, 131072], P(None, ('blk', 'col'))
- new_context_bias: float32 [131072], P(('blk', 'col'))
All inputs are finite; a program needn't handle non-finite values. No bound on the sum of `tile_mask` on one device may be relied on, other than what follows from the above.
Results may differ from a plain program's by a relative error of at most 0.0075.
Values may be sent and summed in bfloat16 or wider, within the bound.
A program may use at most 64 MiB of HBM per device.

v0:
```python
import jax
import jax.numpy as jnp
from jax import lax
from jax.sharding import PartitionSpec as P

RATE = 0.05
XMAX = 100.0
POWER = 0.75


def from_behind(block, axis, distance):
    devices = range(lax.axis_size(axis))
    route = [((i - distance) % len(devices), i) for i in devices]
    return lax.ppermute(block, axis, route)


def adagrad(param, accum, grad):
    accum = accum + grad * grad
    return (param - RATE * grad / jnp.sqrt(accum), accum)


def per_device(word_vectors, word_bias, context_vectors, context_bias, counts, tile_mask):
    width = context_vectors.shape[1]
    tile_rows = tile_mask.shape[1]
    tile_cols = tile_mask.shape[2]
    rows = counts.shape[1]
    side = rows // tile_rows
    strata = counts.shape[0]
    wvec, wbias = (
        lax.all_gather(word_vectors, "col", axis=1, tiled=True),
        lax.all_gather(word_bias, "col", axis=0, tiled=True),
    )
    cvec, cbias = (context_vectors, context_bias)
    cacc = jnp.ones_like(cvec)
    cbacc = jnp.ones_like(cbias)
    wshare, wbshare = (word_vectors, word_bias)
    wacc = jnp.ones_like(wvec)
    wbacc = jnp.ones_like(wbias)
    for stratum in range(strata):
        xval = counts[stratum].astype(jnp.float32)
        tiles = jnp.broadcast_to(
            tile_mask[stratum].astype(jnp.float32)[:, None, :, None],
            (tile_rows, side, tile_cols, side),
        ).reshape(rows, width)
        weight = tiles * jnp.minimum((xval / XMAX) ** POWER, 1.0)
        target = jnp.log(jnp.maximum(xval, 1.0))
        pred = lax.dot_general(
            wvec,
            cvec,
            (((0,), (0,)), ((), ())),
            precision=lax.Precision.HIGHEST,
            preferred_element_type=jnp.float32,
        )
        grads = weight * (pred + wbias[:, None] + cbias[None, :] - target)
        partial_word = lax.dot_general(
            cvec,
            grads,
            (((1,), (1,)), ((), ())),
            precision=lax.Precision.HIGHEST,
            preferred_element_type=jnp.float32,
        )
        partial_bias = jnp.sum(grads, axis=1)
        grad_ctx = jnp.dot(
            wvec, grads, precision=lax.Precision.HIGHEST, preferred_element_type=jnp.float32
        )
        grad_cbias = jnp.sum(grads, axis=0)
        grad_word, grad_wbias = (
            lax.psum(partial_word.astype(jnp.bfloat16), "col").astype(jnp.float32),
            lax.psum(partial_bias.astype(jnp.bfloat16), "col").astype(jnp.float32),
        )
        wvec, wacc = adagrad(wvec, wacc, grad_word)
        wbias, wbacc = adagrad(wbias, wbacc, grad_wbias)
        cvec, cacc = adagrad(cvec, cacc, grad_ctx)
        cbias, cbacc = adagrad(cbias, cbacc, grad_cbias)
        cvec, cbias, cacc, cbacc = from_behind((cvec, cbias, cacc, cbacc), "blk", 1)
    start = lax.axis_index("col") * width
    wshare = lax.dynamic_slice_in_dim(wvec, start, width, 1)
    wbshare = lax.dynamic_slice_in_dim(wbias, start, width, 0)
    return (wshare, wbshare, cvec, cbias)


def solution(mesh):
    in_specs = (
        P(None, ("blk", "col")),
        P(("blk", "col")),
        P(None, ("blk", "col")),
        P(("blk", "col")),
        P(None, "blk", "col"),
        P(None, "blk", "col"),
    )
    out_specs = (
        P(None, ("blk", "col")),
        P(("blk", "col")),
        P(None, ("blk", "col")),
        P(("blk", "col")),
    )
    return jax.shard_map(
        per_device, mesh=mesh, in_specs=in_specs, out_specs=out_specs, check_vma=False
    )
```

profile of v0, /device:TPU:24, one launch (start us, length us, event | category | flops | bytes accessed | tf_op | source)
XLA Modules:
  0.0 701.2 jit_solution(15123664728911088331)
XLA Ops:
  7.2 0.0 copy-start.3
  7.2 0.0 copy-start.5
  7.2 0.0 copy-start.4
  7.2 0.0 all-gather.3.cloned.1.call-start
  7.2 0.7 all-gather.3.cloned.1.call-update
  7.9 0.0 all-reduce.3.cloned.1.call-start
  8.0 0.7 convert_bitcast_fusion
  8.7 0.1 copy.12
  8.8 49.7 %all-gather = f32[8,1,256]{2,1,0:T(1,128)S(1)} all-gather(f32[1,1,256]{2,1,0:T(1,128)} %bitcast.60), channel_id=1, replica_groups=mesh['blk'=64,'col'=8] {'col'}, dimensions={0}, use_global_device_ids=true | all-gather | bytes 9216 | tf_op jit(solution)/shard_map/all_gather | solution.py:31
  58.5 83.8 %all-gather.3.cloned.1.call-done = f32[300,2048]{1,0:T(8,128)} async-done(((f32[300,256]{1,0:T(8,128)}), f32[300,2048]{1,0:T(8,128)}) %all-gather.3.cloned.1.call-update) | async-done | bytes 2457616 | tf_op jit(solution)/shard_map/all_gather | solution.py:30
  142.3 0.6 broadcast_in_dim.12
  142.9 0.0 copy-done.3
  142.9 0.0 copy-done.5
  142.9 0.0 copy-done.4
  142.9 9.1 %fusion.35 = (bf16[2048]{0:T(1024)(128)(2,1)S(1)}, f32[256]{0:T(256)S(1)}, f32[2048,256]{1,0:T(8,128)S(1)}) fusion(f32[256]{0:T(256)S(1)} %copy-done.4, f32[2048]{0:T(1024)S(1)} %bitcast.58, f32[300,2048]{1,0:T(8,128)} %all-gather.3.cloned.1.call-done, f32[300,256]{1,0:T(8,128)S(1)} %copy-done.3, bf16[2,2048,256]{2,1,0:T(8,128)(2,1)S(1)} %copy-done.5, ...), kind=kOutput, calls=%fused_computation.59 | convolution fusion | flops 1893201664 | bytes 8022016 | tf_op jit(solution)/shard_map/dot_general | solution.py:47
  152.0 0.0 copy-start.2
  152.1 1.3 copy-done.2
  153.4 0.0 copy-start
  153.4 3.4 fusion.6
  156.7 0.0 all-reduce.3.cloned.1.call-update
  156.8 0.0 all-reduce.5.cloned.1.call-start
  156.8 0.1 copy.13
  156.9 2.1 collective-permute-start.1
  159.0 0.0 copy-done
  159.0 3.9 fusion.26
  162.9 2.3 collective-permute-start
  165.2 40.3 %psum.29 = bf16[2048]{0:T(1024)(128)(2,1)S(1)} all-reduce(bf16[2048]{0:T(1024)(128)(2,1)S(1)} %get-tuple-element.6), channel_id=1, replica_groups=mesh['blk'=64,'col'=8] {'col'}, use_global_device_ids=true, to_apply=%region_2.0 | all-reduce | flops 2048 | bytes 8192 | tf_op jit(solution)/shard_map/psum | solution.py:69
  205.6 208.3 %all-reduce.3.cloned.1.call-done = bf16[300,2048]{1,0:T(8,128)(2,1)} async-done(((bf16[300,2048]{1,0:T(8,128)(2,1)}), bf16[300,2048]{1,0:T(8,128)(2,1)}) %all-reduce.3.cloned.1.call-update) | async-done | bytes 1228816 | tf_op jit(solution)/shard_map/psum | solution.py:68
  413.9 4.3 fusion.9
  418.2 0.0 copy-start.6
  418.2 0.0 collective-permute-done.1
  418.2 0.0 collective-permute-done
  418.2 0.6 broadcast_in_dim.15
  418.8 1.0 copy-done.6
  419.8 7.4 %fusion.34 = (f32[256]{0:T(256)S(1)}, bf16[2048]{0:T(1024)(128)(2,1)S(1)}, f32[2048,256]{1,0:T(8,128)S(1)}) fusion(f32[256]{0:T(256)S(1)} %collective-permute-done.1, f32[2048]{0:T(1024)S(1)} %get-tuple-element.11, f32[300,2048]{1,0:T(8,128)S(1)} %get-tuple-element.9, f32[300,256]{1,0:T(8,128)S(1)} %collective-permute-done, ...), kind=kOutput, calls=%fused_computation.58 | convolution fusion | flops 1893201664 | bytes 8022016 | tf_op jit(solution)/shard_map/dot_general | solution.py:47
  427.2 0.0 copy-start.1
  427.2 1.3 copy-done.1
  428.5 3.3 convolution_convert_fusion
  431.8 0.0 all-reduce.5.cloned.1.call-update
  431.9 1.9 collective-permute-start.2
  433.8 2.4 collective-permute-start.4
  436.3 12.7 %collective-permute-done.2 = f32[300,256]{1,0:T(8,128)} collective-permute-done((f32[300,256]{1,0:T(8,128)S(1)}, f32[300,256]{1,0:T(8,128)}, u32[]{:S(2)}, u32[]{:S(2)}) %collective-permute-start.2) | collective-permute-done | bytes 307232 | tf_op jit(solution)/shard_map/ppermute | solution.py:14
  448.9 3.8 multiply_subtract_fusion
  452.7 1.9 collective-permute-start.3
  454.7 0.0 collective-permute-done.4
  454.7 1.9 collective-permute-start.5
  456.6 52.0 %psum.31 = bf16[2048]{0:T(1024)(128)(2,1)S(1)} all-reduce(bf16[2048]{0:T(1024)(128)(2,1)S(1)} %get-tuple-element.5), channel_id=1, replica_groups=mesh['blk'=64,'col'=8] {'col'}, use_global_device_ids=true, to_apply=%region_6.0 | all-reduce | flops 2048 | bytes 8192 | tf_op jit(solution)/shard_map/psum | solution.py:69
  508.6 0.6 fusion.31
  509.3 0.0 collective-permute-done.5
  509.3 0.0 collective-permute-done.3
  509.3 182.3 %all-reduce.5.cloned.1.call-done = bf16[300,2048]{1,0:T(8,128)(2,1)} async-done(((bf16[300,2048]{1,0:T(8,128)(2,1)}), bf16[300,2048]{1,0:T(8,128)(2,1)}) %all-reduce.5.cloned.1.call-update) | async-done | bytes 1228816 | tf_op jit(solution)/shard_map/psum | solution.py:68
  691.6 1.8 fusion.23
  693.4 0.7 copy.22
  694.1 0.6 copy.23
  (4 shorter events, 0.1 us)
Async XLA Ops:
  7.2 135.7 %copy-start.3 = (f32[300,256]{1,0:T(8,128)S(1)}, f32[300,256]{1,0:T(8,128)}, u32[]{:S(2)}) copy-start(f32[300,256]{1,0:T(8,128)} %param.8) | copy-start | bytes 921604
  7.2 135.7 %copy-start.5 = (bf16[2,2048,256]{2,1,0:T(8,128)(2,1)S(1)}, bf16[2,2048,256]{2,1,0:T(8,128)(2,1)}, u32[]{:S(2)}) copy-start(bf16[2,2048,256]{2,1,0:T(8,128)(2,1)} %param.10) | copy-start | bytes 6291460
  7.2 135.7 %copy-start.4 = (f32[256]{0:T(256)S(1)}, f32[256]{0:T(256)}, u32[]{:S(2)}) copy-start(f32[256]{0:T(256)} %param.9) | copy-start | bytes 3076
  7.2 135.1 %all-gather.3.cloned.1.call-start = ((), (), s32[]{:S(2)}) async-start(), calls=%async_computation | async-start | bytes 2801664 | tf_op jit(solution)/shard_map/all_gather | solution.py:30
  7.9 406.0 %all-reduce.3.cloned.1.call-start = ((), (), s32[]{:S(2)}) async-start(), calls=%async_computation.1 | async-start | bytes 2490368 | tf_op jit(solution)/shard_map/psum | solution.py:68
  152.0 1.3 copy-start.2
  153.4 5.6 copy-start
  156.8 534.8 %all-reduce.5.cloned.1.call-start = ((), (), s32[]{:S(2)}) async-start(), calls=%async_computation.2 | async-start | bytes 2490368 | tf_op jit(solution)/shard_map/psum | solution.py:68
  156.9 261.3 %collective-permute-start.1 = (f32[256]{0:T(256)S(1)}, f32[256]{0:T(256)S(1)}, u32[]{:S(2)}, u32[]{:S(2)}) collective-permute-start(f32[256]{0:T(256)S(1)} %get-tuple-element.15), channel_id=1, source_target_pairs={{504,0},{0,8},{8,16},{16,24},{24,32},{32,40},{40,48},{48,56},{56,6... | collective-permute-start | bytes 3080 | tf_op jit(solution)/shard_map/ppermute | solution.py:14
  162.9 255.3 %collective-permute-start = (f32[300,256]{1,0:T(8,128)S(1)}, f32[300,256]{1,0:T(8,128)S(1)}, u32[]{:S(2)}, u32[]{:S(2)}) collective-permute-start(f32[300,256]{1,0:T(8,128)S(1)} %get-tuple-element.16), channel_id=1, source_target_pairs={{504,0},{0,8},{8,16},{16,24},{24,32},{32,40},{40,48},{48,56},{56,6... | collective-permute-start | bytes 921608 | tf_op jit(solution)/shard_map/ppermute | solution.py:14
  418.2 1.6 copy-start.6
  427.2 1.3 copy-start.1
  431.9 17.0 %collective-permute-start.2 = (f32[300,256]{1,0:T(8,128)S(1)}, f32[300,256]{1,0:T(8,128)}, u32[]{:S(2)}, u32[]{:S(2)}) collective-permute-start(f32[300,256]{1,0:T(8,128)S(1)} %add_bitcast_fusion), channel_id=1, source_target_pairs={{504,0},{0,8},{8,16},{16,24},{24,32},{32,40},{40,48},{48,56},{56,6... | collective-permute-start | bytes 921608 | tf_op jit(solution)/shard_map/ppermute | solution.py:14
  433.8 20.8 %collective-permute-start.4 = (f32[256]{0:T(256)S(1)}, f32[256]{0:T(256)S(1)}, u32[]{:S(2)}, u32[]{:S(2)}) collective-permute-start(f32[256]{0:T(256)S(1)} %get-tuple-element.14), channel_id=1, source_target_pairs={{504,0},{0,8},{8,16},{16,24},{24,32},{32,40},{40,48},{48,56},{56,6... | collective-permute-start | bytes 3080 | tf_op jit(solution)/shard_map/ppermute | solution.py:14
  452.7 56.6 %collective-permute-start.3 = (f32[300,256]{1,0:T(8,128)S(1)}, f32[300,256]{1,0:T(8,128)S(1)}, u32[]{:S(2)}, u32[]{:S(2)}) collective-permute-start(f32[300,256]{1,0:T(8,128)S(1)} %multiply_subtract_fusion), channel_id=1, source_target_pairs={{504,0},{0,8},{8,16},{16,24},{24,32},{32,40},{40,48},{48,56},{56,6... | collective-permute-start | bytes 921608 | tf_op jit(solution)/shard_map/ppermute | solution.py:14
  454.7 54.6 %collective-permute-start.5 = (f32[256]{0:T(256)S(1)}, f32[256]{0:T(256)S(1)}, u32[]{:S(2)}, u32[]{:S(2)}) collective-permute-start(f32[256]{0:T(256)S(1)} %multiply_subtract_fusion.1), channel_id=1, source_target_pairs={{504,0},{0,8},{8,16},{16,24},{24,32},{32,40},{40,48},{48,56},{56,6... | collective-permute-start | bytes 3080 | tf_op jit(solution)/shard_map/ppermute | solution.py:14
Sparse Core Ops, SparseCore 0:
  11.1 131.1 all-gather.2
  156.9 256.9 all-reduce.2
  432.0 259.5 all-reduce.4
where the time goes:
time: 704 us; the launch traced here: 701 us
  waiting for transfers between devices  488 us (69%)
  blocking collectives  142 us (20%)
  matrix products  30.9 us (4%)
  between operations  13.9 us (2%)
  starting transfers between devices  12.7 us (2%)
  other arithmetic  7.51 us (1%)
    psum x2, waiting for transfers between devices, per_device(): lax.psum(partial_word.astype(jnp.bfloat16), 'col').astype(jnp.float32)  391 us
    psum x2, blocking collectives, per_device(): lax.psum(partial_bias.astype(jnp.bfloat16), 'col').astype(jnp.float32)  92.4 us
    all_gather x1, waiting for transfers between devices, per_device(): lax.all_gather(word_vectors, 'col', axis=1, tiled=True)  83.8 us
    all_gather x1, blocking collectives, per_device(): lax.all_gather(word_bias, 'col', axis=0, tiled=True)  49.7 us
    dot_general x2, matrix products, per_device(): lax.dot_general(wvec, cvec, (((0,), (0,)), ((), ())), precision=lax.Preci...  16.6 us
  transfers between devices with their start and end apart: 9, of which 4 were waited for; matrix products, arithmetic and copies ran while one was open for 2% of the time, Pallas kernels for 0%

commit v1 on v0

v1 whole, which is shorter than its diff:
```python
import functools
import math

import jax
import jax.numpy as jnp
from jax import lax
from jax.experimental import pallas as pl
from jax.experimental.pallas import tpu as pltpu
from jax.sharding import PartitionSpec as P

RATE = 0.05
XMAX = 100.0
POWER = 0.75
MESH = pl.DeviceIdType.MESH
F32 = jnp.float32
BF16 = jnp.bfloat16
N_Y = 4
SIDE = 128

ORDER = (
    ("prep", 0, 0, 0), ("unit", 0, 0, 0, 0), ("prep", 0, 0, 1), ("unit", 0, 0, 1, 0),
    ("cgrad", 0, 0, 0), ("fwd", 0, 0, 0), ("unit", 0, 0, 0, 1), ("unit", 0, 0, 0, 3),
    ("fwd", 0, 0, 1), ("unit", 0, 0, 1, 1), ("unit", 0, 0, 1, 3), ("cearly",),
    ("unit", 0, 0, 0, 2), ("cgrad", 0, 0, 1), ("cgrad", 0, 0, 3), ("relay", 0, 0),
    ("relay", 0, 1), ("prep", 0, 1, 0), ("prep", 0, 1, 1), ("unit", 0, 0, 1, 2),
    ("cgrad", 0, 0, 2), ("prep", 1, 1, 0), ("prep", 1, 1, 1), ("prep", 1, 0, 0),
    ("prep", 1, 0, 1), ("half", 0, 0, 0), ("half", 0, 0, 1), ("words", 0), ("words", 1),
    ("unit", 0, 1, 0, 0), ("unit", 0, 1, 1, 0), ("cgrad", 0, 1, 0), ("fwd", 0, 1, 0),
    ("unit", 0, 1, 0, 1), ("unit", 0, 1, 0, 3), ("fwd", 0, 1, 1), ("unit", 0, 1, 1, 1),
    ("unit", 0, 1, 1, 3), ("cgrad", 0, 1, 1), ("relay", 2, 0), ("unit", 0, 1, 0, 2),
    ("relay", 2, 1), ("cgrad", 0, 1, 3), ("unit", 0, 1, 1, 2), ("cgrad", 0, 1, 2), ("con",),
    ("half", 0, 1, 0), ("half", 0, 1, 1), ("update", 1, 0), ("update", 1, 1), ("cin",),
    ("unit", 1, 1, 0, 0), ("unit", 1, 1, 1, 0), ("fwd", 1, 1, 0), ("unit", 1, 1, 0, 1),
    ("unit", 1, 1, 0, 3), ("fwd", 1, 1, 1), ("unit", 1, 1, 1, 1), ("unit", 1, 1, 1, 3),
    ("cgrad", 1, 1, 0), ("relay", 1, 0), ("unit", 1, 1, 0, 2), ("cgrad", 1, 1, 1),
    ("relay", 1, 1), ("cgrad", 1, 1, 3), ("unit", 1, 1, 1, 2), ("cgrad", 1, 1, 2),
    ("half", 1, 1, 0), ("half", 1, 1, 1), ("update", 0, 0), ("unit", 1, 0, 0, 0),
    ("update", 0, 1), ("unit", 1, 0, 1, 0), ("cgrad", 1, 0, 0), ("fwd", 1, 0, 0),
    ("unit", 1, 0, 0, 1), ("unit", 1, 0, 0, 3), ("fwd", 1, 0, 1), ("unit", 1, 0, 1, 1),
    ("unit", 1, 0, 1, 3), ("cgrad", 1, 0, 1), ("relay", 3, 0), ("unit", 1, 0, 0, 2),
    ("cgrad", 1, 0, 3), ("relay", 3, 1), ("unit", 1, 0, 1, 2), ("cgrad", 1, 0, 2), ("clast",),
    ("half", 1, 0, 0), ("half", 1, 0, 1), ("result", 0), ("cresult",), ("result", 1),
)


def with_bias_rows(full, dim, first):
    top = dim - dim % 8
    tail = full[top:]
    at = dim % 8
    bias = tail[at + first:at + first + 1]
    high = bias.astype(BF16).astype(F32)
    low = bias - high
    row = lax.broadcasted_iota(jnp.int32, tail.shape, 0)
    other = 2 - first
    tail = jnp.where(row == at + first, high, tail)
    tail = jnp.where(row == at + first + 1, low, tail)
    tail = jnp.where((row >= at + other) & (row <= at + other + 1), 1.0, tail)
    return jnp.concatenate([full[:top], tail], axis=0).astype(BF16)


def kernel(nb, dim, wv, wb, cv, cb, cnt, msk, ow, owb, oc, ocb,
           wv_in, wb_in, cv_in, cb_in, cnt_in, in_s,
           wbuf, psend, pbuf, hsend, hrecv, zbuf, hsum, wp, wacc, hp, hbf, hbt, hprev, gacc,
           cacc, csend, crecv, fsend, frecv, wgt, wtl, gbuf,
           ag_s, ag_r, rs_s, rs_r, z1_s, z1_r, z2_s, z2_r, cx_s, cx_r):
    b = lax.axis_index("blk")
    c = lax.axis_index("col")
    y = lax.div(c, 2)
    zh = lax.rem(c, 2)
    upper = lax.div(b, nb // 2)
    across = lax.rem(b + nb // 2, nb)
    z_col = (y * 2 + lax.rem(zh + upper, 2), y * 2 + lax.rem(zh + 1 - upper, 2))
    nxt = lax.rem(b + 1, nb)
    prv = lax.rem(b + nb - 1, nb)
    width = wv.shape[1]
    halves = width // SIDE
    top, at = dim - dim % 8, dim % 8

    def remote(src, dst, ssem, rsem, blk, col):
        return pltpu.make_async_remote_copy(
            src_ref=src, dst_ref=dst, send_sem=ssem, recv_sem=rsem,
            device_id=(blk, col), device_id_type=MESH)

    def y_of(k):
        return lax.rem(y + k, N_Y)

    def mate(k):
        return y_of(k) * 2 + zh

    def ag_copy(t, p, f, k):
        return remote(wbuf.at[t, p, y, f], wbuf.at[t, p, y, f],
                      ag_s.at[t, p, f, k], ag_r.at[t, p, f, y], b, mate(k))

    def ag_forward(t, p, f):
        ys, to = (y_of(3), 1) if f == 0 else (y_of(1), 3)
        return remote(wbuf.at[t, p, ys, f], wbuf.at[t, p, ys, f],
                      ag_s.at[t, p, f, 2], ag_r.at[t, p, f, ys], b, mate(to))

    def ag_wait(t, p, f, k):
        yk = y_of(k)
        remote(wbuf.at[t, p, yk, f], wbuf.at[t, p, yk, f],
               ag_s.at[t, p, f, k], ag_r.at[t, p, f, yk], b, mate(k)).wait_recv()

    def rs_copy(t, p, f, k):
        return remote(psend.at[t, p, y_of(k), f], pbuf.at[t, p, y, f],
                      rs_s.at[t, p, f, k], rs_r.at[t, p, f, y], b, mate(k))

    def rs_wait(t, p, f, k):
        yk = y_of(k)
        remote(psend.at[t, p, yk, f], pbuf.at[t, p, yk, f],
               rs_s.at[t, p, f, k], rs_r.at[t, p, f, yk], b, mate(k)).wait_recv()

    def z_ends(i, f):
        return ((wbuf.at[0, 0, y, f], wbuf.at[0, 1, y, f]),
                (hsend.at[0, 1, f], hrecv.at[0, 0, f]),
                (hsend.at[0, 0, f], hrecv.at[0, 1, f]),
                (hsend.at[1, 1, f], hrecv.at[1, 0, f]))[i]

    def z_first(i, f):
        return remote(z_ends(i, f)[0], zbuf.at[i, f], z1_s.at[i, f], z1_r.at[i, f], across, z_col[f])

    def z_second(i, f):
        return remote(zbuf.at[i, f], z_ends(i, f)[1], z2_s.at[i, f], z2_r.at[i, f],
                      across, z_col[f])

    def relay(i, f):
        z_first(i, f).wait_recv()
        z_second(i, f).start()

    def cx_copy(i):
        src, dst = ((hbf.at[0], hprev), (csend, crecv), (fsend, frecv))[i]
        return remote(src, dst, cx_s.at[i], cx_r.at[i], nxt, c)

    def all_gather(t, p, f):
        for k in ((1, 3) if f == 0 else (3, 1)):
            ag_copy(t, p, f, k).start()

    def shard_of(p, j):
        return y_of(j) * 2 + (zh if p == 0 else 1 - zh)

    def prep(t, p, f):
        def step(k, carry):
            tile_row = shard_of(p, k) * halves + f
            rows = pl.ds(pl.multiple_of(tile_row * SIDE, SIDE), SIDE)
            for q in range(halves):
                cols = pl.ds(q * SIDE, SIDE)
                logx = jnp.log(cnt_in[t, rows, cols].astype(F32).T)
                weight = jnp.minimum(jnp.exp(POWER * logx - POWER * math.log(XMAX)), 1.0)
                weight = weight * msk[t, q, tile_row].astype(F32)
                wgt[t, p, k, f, cols, :] = weight
                wtl[t, p, k, f, cols, :] = weight * jnp.maximum(logx, 0.0)
            return carry

        lax.fori_loop(0, N_Y, step, 0)

    def fwd(t, p, f):
        ag_wait(t, p, f, 3 if f == 0 else 1)
        ag_forward(t, p, f).start()

    def unit(t, p, f, k):
        if k == 2 or k == (1 if f == 0 else 3):
            ag_wait(t, p, f, k)
        yk = y_of(k)
        pred = jnp.dot(hbt[t], wbuf[t, p, yk, f], preferred_element_type=F32)
        g = (wgt[t, p, k, f] * pred - wtl[t, p, k, f]).astype(BF16)
        gbuf[t, p, k, :, f * SIDE:(f + 1) * SIDE] = g
        psend[t, p, yk, f] = jnp.dot(hbf[t], g, preferred_element_type=F32).astype(BF16)
        if k:
            rs_copy(t, p, f, k).start()

    def cgrad(t, p, k):
        yk = y_of(k)
        words = jnp.concatenate([wbuf[t, p, yk, f] for f in range(halves)], axis=1)
        gacc[t] += lax.dot_general(words, gbuf[t, p, k], (((1,), (1,)), ((), ())),
                                   preferred_element_type=F32)

    def half(t, p, f):
        total = psend[t, p, y, f].astype(F32)
        for k in (1, 3, 2):
            rs_wait(t, p, f, k)
            total = total + pbuf[t, p, y_of(k), f].astype(F32)
        hsum[t, p, f] = total
        if (t, p) != (1, 0):
            hsend[t, p, f] = total.astype(BF16)
            z_first({(0, 0): 2, (0, 1): 1, (1, 1): 3}[t, p], f).start()

    def partner_words(f):
        z_second(0, f).wait_recv()
        all_gather(0, 1, f)

    def update(p, f):
        z_second(1 + p, f).wait_recv()
        grad = hsum[0, p, f] + hrecv[0, p, f].astype(F32)
        acc = 1.0 + grad * grad
        words = wp[f] if p == 0 else with_whole_bias(wbuf[0, 1, y, f].astype(F32), 0)
        words = words - RATE * grad * lax.rsqrt(acc)
        if p == 0:
            wacc[f] = acc
            wp[f] = words
        wbuf[1, p, y, f] = with_bias_rows(words, dim, 0)
        all_gather(1, p, f)

    def result(f):
        z_second(3, f).wait_recv()
        grad = hsum[1, 0, f] + hrecv[1, 0, f].astype(F32)
        words = wp[f] - RATE * grad * lax.rsqrt(wacc[f] + grad * grad)
        lanes = slice(f * SIDE, (f + 1) * SIDE)
        ow[:, lanes] = words[0:dim]
        owb[:, lanes] = words[dim:dim + 1]

    def context_early():
        cx_copy(0).start()

    def context_on():
        csend[...] = gacc[0].astype(BF16)
        cx_copy(1).start()

    def context_in():
        cx_copy(0).wait_recv()
        cx_copy(1).wait_recv()
        grad = crecv[...].astype(F32)
        acc = 1.0 + grad * grad
        cacc[...] = acc
        held = with_whole_bias(hprev[...].astype(F32), 2) - RATE * grad * lax.rsqrt(acc)
        hp[...] = held
        hbf[1] = with_bias_rows(held, dim, 2)
        hbt[1] = hbf[1].astype(F32).T.astype(BF16)

    def context_last():
        grad = gacc[1]
        held = hp[...] - RATE * grad * lax.rsqrt(cacc[...] + grad * grad)
        fsend[...] = with_bias_rows(held, dim, 2)
        cx_copy(2).start()

    def context_result():
        cx_copy(2).wait_recv()
        held = frecv[...].astype(F32)
        oc[...] = held[0:dim]
        ocb[...] = held[dim + 2:dim + 3] + held[dim + 3:dim + 4]

    def with_whole_bias(full, first):
        end = full[top:]
        i = at + first
        row = lax.broadcasted_iota(jnp.int32, end.shape, 0)
        end = jnp.where(row == i, end[i:i + 1] + end[i + 1:i + 2], end)
        return jnp.concatenate([full[:top], end], axis=0)

    barrier = pltpu.get_barrier_semaphore()
    others = [(b, mate(k)) for k in (1, 2, 3)] + [
        (across, z_col[0]), (across, z_col[1]), (nxt, c), (prv, c)]
    for other in others:
        pl.semaphore_signal(barrier, inc=1, device_id=other, device_id_type=MESH)

    loads = [pltpu.make_async_copy(src, dst, in_s.at[i]) for i, (src, dst) in enumerate(
        ((wv, wv_in), (wb, wb_in), (cnt, cnt_in), (cv, cv_in), (cb, cb_in)))]
    for load in loads:
        load.start()

    loads[0].wait()
    loads[1].wait()
    for f in range(halves):
        lanes = slice(f * SIDE, (f + 1) * SIDE)
        wp[f, 0:dim, :] = wv_in[:, lanes]
        wp[f, dim:dim + 1, :] = wb_in[:, lanes]
        wp[f, dim + 1:dim + 4, :] = jnp.zeros((3, SIDE), F32)
        wbuf[0, 0, y, f] = with_bias_rows(wp[f], dim, 0)

    pl.semaphore_wait(barrier, len(others))

    for f in range(halves):
        z_first(0, f).start()
        all_gather(0, 0, f)
    for load in loads[2:]:
        load.wait()
    hp[0:dim, :] = cv_in[...]
    hp[dim:dim + 2, :] = jnp.zeros((2, width), F32)
    hp[dim + 2:dim + 3, :] = cb_in[...]
    hp[dim + 3:dim + 4, :] = jnp.zeros((1, width), F32)
    hbf[0] = with_bias_rows(hp[...], dim, 2)
    hbt[0] = hbf[0].astype(F32).T.astype(BF16)
    gacc[...] = jnp.zeros_like(gacc)

    steps = dict(relay=relay, prep=prep, unit=unit, fwd=fwd, half=half, cgrad=cgrad, words=partner_words,
                 update=update, result=result, cearly=context_early, con=context_on, cin=context_in,
                 clast=context_last, cresult=context_result)
    for name, *which in ORDER:
        steps[name](*which)

    for f in range(halves):
        for i in range(4):
            z_first(i, f).wait_send()
            z_second(i, f).wait_send()
        for t in range(2):
            for p in range(2):
                ag_forward(t, p, f).wait_send()
                ag_copy(t, p, f, 1).wait_send()
                ag_copy(t, p, f, 3).wait_send()
                for k in (1, 2, 3):
                    rs_copy(t, p, f, k).wait_send()
    for i in range(3):
        cx_copy(i).wait_send()


def copy_out(*refs):
    n = len(refs) // 2
    sems = refs[-1]
    copies = [pltpu.make_async_copy(refs[i], refs[n + i], sems.at[i]) for i in range(n)]
    for copy in copies:
        copy.start()
    for copy in copies:
        copy.wait()


def per_device(nb, word_vectors, word_bias, context_vectors, context_bias, counts, tile_mask):
    dim, width = word_vectors.shape
    tall, halves = dim + 4, width // SIDE
    vmem = pl.BlockSpec(memory_space=pltpu.VMEM)
    hbm = pl.BlockSpec(memory_space=pltpu.HBM)
    dma = pltpu.SemaphoreType.DMA
    piece = (halves, tall, SIDE)
    shapes = tuple(pltpu.VMEM((n, width), F32) for n in (dim, 1, dim, 1))
    results = pl.pallas_call(
        functools.partial(kernel, nb, dim),
        out_shape=shapes,
        in_specs=[hbm] * 5 + [pl.BlockSpec(memory_space=pltpu.SMEM)],
        out_specs=(vmem,) * 4,
        scratch_shapes=[
            pltpu.VMEM((dim, width), F32),
            pltpu.VMEM((1, width), F32),
            pltpu.VMEM((dim, width), F32),
            pltpu.VMEM((1, width), F32),
            pltpu.VMEM(counts.shape, BF16),
            dma((5,)),
            pltpu.VMEM((2, 2, N_Y) + piece, BF16),
            pltpu.VMEM((2, 2, N_Y) + piece, BF16),
            pltpu.VMEM((2, 2, N_Y) + piece, BF16),
            pltpu.VMEM((2, 2) + piece, BF16),
            pltpu.VMEM((2, 2) + piece, BF16),
            pltpu.VMEM((4,) + piece, BF16),
            pltpu.VMEM((2, 2) + piece, F32),
            pltpu.VMEM(piece, F32),
            pltpu.VMEM(piece, F32),
            pltpu.VMEM((tall, width), F32),
            pltpu.VMEM((2, tall, width), BF16),
            pltpu.VMEM((2, width, tall), BF16),
            pltpu.VMEM((tall, width), BF16),
            pltpu.VMEM((2, tall, width), F32),
            pltpu.VMEM((tall, width), F32),
            pltpu.VMEM((tall, width), BF16),
            pltpu.VMEM((tall, width), BF16),
            pltpu.VMEM((tall, width), BF16),
            pltpu.VMEM((tall, width), BF16),
            pltpu.VMEM((2, 2, N_Y, halves, width, SIDE), F32),
            pltpu.VMEM((2, 2, N_Y, halves, width, SIDE), F32),
            pltpu.VMEM((2, 2, N_Y, width, width), BF16),
            dma((2, 2, halves, N_Y)), dma((2, 2, halves, N_Y)),
            dma((2, 2, halves, N_Y)), dma((2, 2, halves, N_Y)),
            dma((4, halves)), dma((4, halves)),
            dma((4, halves)), dma((4, halves)),
            dma((3,)), dma((3,)),
        ],
        compiler_params=pltpu.CompilerParams(
            collective_id=0, has_side_effects=True, vmem_limit_bytes=60 * 1024 * 1024),
        cost_estimate=pl.CostEstimate(
            flops=2 * 6 * tall * counts.shape[1] * width, transcendentals=2 * counts.size,
            bytes_accessed=2 * counts.size + 16 * dim * width),
    )(word_vectors, word_bias[None], context_vectors, context_bias[None], counts,
      tile_mask.transpose(0, 2, 1))
    ow, owb, oc, ocb = pl.pallas_call(
        copy_out, out_shape=tuple(jax.ShapeDtypeStruct(s.shape, F32) for s in shapes),
        in_specs=[vmem] * 4, out_specs=(hbm,) * 4,
        scratch_shapes=[dma((4,))],
        compiler_params=pltpu.CompilerParams(vmem_limit_bytes=4 * 1024 * 1024),
        cost_estimate=pl.CostEstimate(
            flops=0, transcendentals=0, bytes_accessed=16 * dim * width),
    )(*results)
    return ow, owb[0], oc, ocb[0]


def solution(mesh):
    spec = P(None, ("blk", "col"))
    line = P(("blk", "col"))
    grid = P(None, "blk", "col")
    return jax.shard_map(
        functools.partial(per_device, mesh.shape["blk"]), mesh=mesh,
        in_specs=(spec, line, spec, line, grid, grid),
        out_specs=(spec, line, spec, line), check_vma=False)
```

time: 704 us -> 93.5 us (0.13)
  waiting for transfers between devices: 488 us -> 0 us
  blocking collectives: 142 us -> 0 us
  Pallas kernels: 0 us -> 92.7 us
  matrix products: 30.9 us -> 0 us
  between operations: 13.9 us -> 0.64 us
  starting transfers between devices: 12.7 us -> 0 us
  other arithmetic: 7.51 us -> 0 us
    psum x2 -> x0, waiting for transfers between devices: 391 us -> none  [per_device(): lax.psum(partial_word.astype(jnp.bfloat16), 'col').astype(jnp.float32)]
    pallas_call x0 -> x2, Pallas kernels: none -> 92.7 us  [the longest x1 91.8 us: per_device(): pl.pallas_call(functools.partial(kernel, nb, dim), out_shape=shapes, in_s...]
    psum x2 -> x0, blocking collectives: 92.4 us -> none  [per_device(): lax.psum(partial_bias.astype(jnp.bfloat16), 'col').astype(jnp.float32)]
    all_gather x1 -> x0, waiting for transfers between devices: 83.8 us -> none  [per_device(): lax.all_gather(word_vectors, 'col', axis=1, tiled=True)]
    all_gather x1 -> x0, blocking collectives: 49.7 us -> none  [per_device(): lax.all_gather(word_bias, 'col', axis=0, tiled=True)]
    dot_general x6 -> x0, matrix products: 30.9 us -> none  [the longest x2 16.6 us: per_device(): lax.dot_general(wvec, cvec, (((0,), (0,)), ((), ())), precision=lax.Preci...]
    ppermute x6 -> x0, waiting for transfers between devices: 12.7 us -> none  [from_behind(): return lax.ppermute(block, axis, route)]
    ppermute x6 -> x0, starting transfers between devices: 12.6 us -> none  [from_behind(): return lax.ppermute(block, axis, route)]
  transfers between devices with their start and end apart: 9 -> 0, of which waited for: 4 -> 0; matrix products, arithmetic and copies ran while one was open for 2% -> 0% of each run, Pallas kernels for 0% -> 0%
where the time goes in v1:
time: 93.5 us; the launch traced here: 93.3 us
  Pallas kernels  92.7 us (99%)
    pallas_call x1, Pallas kernels, per_device(): pl.pallas_call(functools.partial(kernel, nb, dim), out_shape=shapes, in_s...  91.8 us

profile of v1, /device:TPU:24, one launch (start us, length us, event | category | flops | bytes accessed | tf_op | source)
XLA Modules:
  0.0 93.3 jit_solution(3992084070272650315)
XLA Ops:
  0.6 91.8 %shard_map.93 = (f32[300,256]{1,0:T(8,128)S(1)}, f32[1,256]{1,0:T(1,128)S(1)}, f32[300,256]{1,0:T(8,128)S(1)}, f32[1,256]{1,0:T(1,128)S(1)}) custom-call(f32[300,256]{1,0:T(8,128)} %wv.1, f32[1,256]{1,0:T(1,128)} %bitcast.6, f32[300,256]{1,0:T(8,128)} %cv.1, f32[1,256]{1,0:T(1,128)} %bitcast.7, bf16[2,2048,256]{2,1,0:T(8,128)(2,1)} %cnt.1, s32[2,2,16]{2,1,0:T(2,128)} %bitcast.5), custom_call_target="tpu_custom_call" | custom-call | flops 1912602624 | bytes 3325952 | tf_op jit(solution)/shard_map/pallas_call | solution.py:322
  92.5 0.9 shard_map.94

commit v2 on v1

--- a/solution.py
+++ b/solution.py
@@ -18,28 +18,24 @@
 SIDE = 128
 
 ORDER = (
-    ("prep", 0, 0, 0), ("unit", 0, 0, 0, 0), ("prep", 0, 0, 1), ("unit", 0, 0, 1, 0),
-    ("cgrad", 0, 0, 0), ("fwd", 0, 0, 0), ("unit", 0, 0, 0, 1), ("unit", 0, 0, 0, 3),
-    ("fwd", 0, 0, 1), ("unit", 0, 0, 1, 1), ("unit", 0, 0, 1, 3), ("cearly",),
-    ("unit", 0, 0, 0, 2), ("cgrad", 0, 0, 1), ("cgrad", 0, 0, 3), ("relay", 0, 0),
-    ("relay", 0, 1), ("prep", 0, 1, 0), ("prep", 0, 1, 1), ("unit", 0, 0, 1, 2),
-    ("cgrad", 0, 0, 2), ("prep", 1, 1, 0), ("prep", 1, 1, 1), ("prep", 1, 0, 0),
-    ("prep", 1, 0, 1), ("half", 0, 0, 0), ("half", 0, 0, 1), ("words", 0), ("words", 1),
-    ("unit", 0, 1, 0, 0), ("unit", 0, 1, 1, 0), ("cgrad", 0, 1, 0), ("fwd", 0, 1, 0),
-    ("unit", 0, 1, 0, 1), ("unit", 0, 1, 0, 3), ("fwd", 0, 1, 1), ("unit", 0, 1, 1, 1),
-    ("unit", 0, 1, 1, 3), ("cgrad", 0, 1, 1), ("relay", 2, 0), ("unit", 0, 1, 0, 2),
-    ("relay", 2, 1), ("cgrad", 0, 1, 3), ("unit", 0, 1, 1, 2), ("cgrad", 0, 1, 2), ("con",),
-    ("half", 0, 1, 0), ("half", 0, 1, 1), ("update", 1, 0), ("update", 1, 1), ("cin",),
-    ("unit", 1, 1, 0, 0), ("unit", 1, 1, 1, 0), ("fwd", 1, 1, 0), ("unit", 1, 1, 0, 1),
-    ("unit", 1, 1, 0, 3), ("fwd", 1, 1, 1), ("unit", 1, 1, 1, 1), ("unit", 1, 1, 1, 3),
-    ("cgrad", 1, 1, 0), ("relay", 1, 0), ("unit", 1, 1, 0, 2), ("cgrad", 1, 1, 1),
-    ("relay", 1, 1), ("cgrad", 1, 1, 3), ("unit", 1, 1, 1, 2), ("cgrad", 1, 1, 2),
-    ("half", 1, 1, 0), ("half", 1, 1, 1), ("update", 0, 0), ("unit", 1, 0, 0, 0),
-    ("update", 0, 1), ("unit", 1, 0, 1, 0), ("cgrad", 1, 0, 0), ("fwd", 1, 0, 0),
-    ("unit", 1, 0, 0, 1), ("unit", 1, 0, 0, 3), ("fwd", 1, 0, 1), ("unit", 1, 0, 1, 1),
-    ("unit", 1, 0, 1, 3), ("cgrad", 1, 0, 1), ("relay", 3, 0), ("unit", 1, 0, 0, 2),
-    ("cgrad", 1, 0, 3), ("relay", 3, 1), ("unit", 1, 0, 1, 2), ("cgrad", 1, 0, 2), ("clast",),
-    ("half", 1, 0, 0), ("half", 1, 0, 1), ("result", 0), ("cresult",), ("result", 1),
+    ("cearly",), ("prep", 0, 0, 0), ("prep", 0, 0, 1), ("prep", 0, 1, 0), ("fwd", 0, 0, 0),
+    ("near", 0, 0, 0), ("fwd", 0, 0, 1), ("near", 0, 0, 1), ("cgrad", 0, 0, 0, 0),
+    ("far", 0, 0, 0), ("relay", 0, 0), ("relay", 0, 1), ("cgrad", 0, 0, 1, 0),
+    ("cgrad", 0, 0, 0, 1), ("prep", 0, 1, 1), ("far", 0, 0, 1), ("cgrad", 0, 0, 1, 1),
+    ("prep", 1, 1, 0), ("prep", 1, 1, 1), ("half", 0, 0, 0), ("prep", 1, 0, 0), ("half", 0, 0, 1),
+    ("words", 0), ("words", 1), ("prep", 1, 0, 1), ("fwd", 0, 1, 0), ("near", 0, 1, 0),
+    ("cgrad", 0, 1, 0, 0), ("fwd", 0, 1, 1), ("near", 0, 1, 1), ("relay", 2, 0), ("far", 0, 1, 0),
+    ("relay", 2, 1), ("cgrad", 0, 1, 1, 0), ("cgrad", 0, 1, 0, 1), ("far", 0, 1, 1),
+    ("cgrad", 0, 1, 1, 1), ("con",), ("half", 0, 1, 0), ("update", 1, 0), ("half", 0, 1, 1),
+    ("update", 1, 1), ("drain", 0, 0), ("fwd", 1, 1, 0), ("cin",), ("near", 1, 1, 0),
+    ("fwd", 1, 1, 1), ("near", 1, 1, 1), ("relay", 1, 0), ("far", 1, 1, 0), ("relay", 1, 1),
+    ("cgrad", 1, 1, 0, 0), ("cgrad", 1, 1, 1, 0), ("cgrad", 1, 1, 0, 1), ("far", 1, 1, 1),
+    ("cgrad", 1, 1, 1, 1), ("half", 1, 1, 0), ("update", 0, 0), ("half", 1, 1, 1),
+    ("update", 0, 1), ("drain", 0, 1), ("fwd", 1, 0, 0), ("near", 1, 0, 0), ("cgrad", 1, 0, 0, 0),
+    ("fwd", 1, 0, 1), ("near", 1, 0, 1), ("far", 1, 0, 0), ("relay", 3, 0), ("cgrad", 1, 0, 1, 0),
+    ("cgrad", 1, 0, 0, 1), ("relay", 3, 1), ("far", 1, 0, 1), ("cgrad", 1, 0, 1, 1), ("clast",),
+    ("drain", 1, 1), ("half", 1, 0, 0), ("half", 1, 0, 1), ("drain", 1, 0), ("result", 0),
+    ("cresult",), ("result", 1),
 )
 
 
@@ -157,22 +153,40 @@
         ag_wait(t, p, f, 3 if f == 0 else 1)
         ag_forward(t, p, f).start()
 
-    def unit(t, p, f, k):
-        if k == 2 or k == (1 if f == 0 else 3):
-            ag_wait(t, p, f, k)
-        yk = y_of(k)
-        pred = jnp.dot(hbt[t], wbuf[t, p, yk, f], preferred_element_type=F32)
-        g = (wgt[t, p, k, f] * pred - wtl[t, p, k, f]).astype(BF16)
-        gbuf[t, p, k, :, f * SIDE:(f + 1) * SIDE] = g
-        psend[t, p, yk, f] = jnp.dot(hbf[t], g, preferred_element_type=F32).astype(BF16)
-        if k:
-            rs_copy(t, p, f, k).start()
-
-    def cgrad(t, p, k):
-        yk = y_of(k)
-        words = jnp.concatenate([wbuf[t, p, yk, f] for f in range(halves)], axis=1)
-        gacc[t] += lax.dot_general(words, gbuf[t, p, k], (((1,), (1,)), ((), ())),
+    def pair(t, p, f, ks):
+        return jnp.concatenate([wbuf[t, p, y_of(k), f] for k in ks], axis=1)
+
+    def products(t, p, f, ks):
+        both = [jnp.concatenate([ref[t, p, k, f] for k in ks], axis=1) for ref in (wgt, wtl)]
+        pred = jnp.dot(hbt[t], pair(t, p, f, ks), preferred_element_type=F32)
+        g = (both[0] * pred - both[1]).astype(BF16)
+        gbuf[t, p, f, int(0 in ks)] = g
+        part = jnp.dot(hbf[t], g, preferred_element_type=F32).astype(BF16)
+        for i, k in enumerate(ks):
+            psend[t, p, y_of(k), f] = part[:, i * SIDE:(i + 1) * SIDE]
+            if k:
+                rs_copy(t, p, f, k).start()
+
+    def near(t, p, f):
+        ag_wait(t, p, f, 1 if f == 0 else 3)
+        products(t, p, f, (1, 3))
+
+    def far(t, p, f):
+        ag_wait(t, p, f, 2)
+        products(t, p, f, (2, 0))
+
+    def cgrad(t, p, f, i):
+        words = pair(t, p, f, ((1, 3), (2, 0))[i])
+        gacc[t] += lax.dot_general(words, gbuf[t, p, f, i], (((1,), (1,)), ((), ())),
                                    preferred_element_type=F32)
+
+    def drain(t, p):
+        for f in range(halves):
+            ag_forward(t, p, f).wait_send()
+            ag_copy(t, p, f, 1).wait_send()
+            ag_copy(t, p, f, 3).wait_send()
+            for k in (1, 2, 3):
+                rs_copy(t, p, f, k).wait_send()
 
     def half(t, p, f):
         total = psend[t, p, y, f].astype(F32)
@@ -280,7 +294,7 @@
     hbt[0] = hbf[0].astype(F32).T.astype(BF16)
     gacc[...] = jnp.zeros_like(gacc)
 
-    steps = dict(relay=relay, prep=prep, unit=unit, fwd=fwd, half=half, cgrad=cgrad, words=partner_words,
+    steps = dict(relay=relay, prep=prep, near=near, far=far, fwd=fwd, drain=drain, half=half, cgrad=cgrad, words=partner_words,
                  update=update, result=result, cearly=context_early, con=context_on, cin=context_in,
                  clast=context_last, cresult=context_result)
     for name, *which in ORDER:
@@ -290,13 +304,6 @@
         for i in range(4):
             z_first(i, f).wait_send()
             z_second(i, f).wait_send()
-        for t in range(2):
-            for p in range(2):
-                ag_forward(t, p, f).wait_send()
-                ag_copy(t, p, f, 1).wait_send()
-                ag_copy(t, p, f, 3).wait_send()
-                for k in (1, 2, 3):
-                    rs_copy(t, p, f, k).wait_send()
     for i in range(3):
         cx_copy(i).wait_send()
 
@@ -352,7 +359,7 @@
             pltpu.VMEM((tall, width), BF16),
             pltpu.VMEM((2, 2, N_Y, halves, width, SIDE), F32),
             pltpu.VMEM((2, 2, N_Y, halves, width, SIDE), F32),
-            pltpu.VMEM((2, 2, N_Y, width, width), BF16),
+            pltpu.VMEM((2, 2, halves, 2, width, 2 * SIDE), BF16),
             dma((2, 2, halves, N_Y)), dma((2, 2, halves, N_Y)),
             dma((2, 2, halves, N_Y)), dma((2, 2, halves, N_Y)),
             dma((4, halves)), dma((4, halves)),

time: 93.5 us -> 93.1 us (level)
  no operation moved by 1% of the time
where the time goes in v2:
time: 93.1 us; the launch traced here: 92.9 us
  Pallas kernels  92.3 us (99%)
    pallas_call x1, Pallas kernels, per_device(): pl.pallas_call(functools.partial(kernel, nb, dim), out_shape=shapes, in_s...  91.4 us

profile of v2, /device:TPU:24, one launch (start us, length us, event | category | flops | bytes accessed | tf_op | source)
XLA Modules:
  0.0 92.9 jit_solution(3778571449366287755)
XLA Ops:
  0.6 91.4 %shard_map.93 = (f32[300,256]{1,0:T(8,128)S(1)}, f32[1,256]{1,0:T(1,128)S(1)}, f32[300,256]{1,0:T(8,128)S(1)}, f32[1,256]{1,0:T(1,128)S(1)}) custom-call(f32[300,256]{1,0:T(8,128)} %wv.1, f32[1,256]{1,0:T(1,128)} %bitcast.6, f32[300,256]{1,0:T(8,128)} %cv.1, f32[1,256]{1,0:T(1,128)} %bitcast.7, bf16[2,2048,256]{2,1,0:T(8,128)(2,1)} %cnt.1, s32[2,2,16]{2,1,0:T(2,128)} %bitcast.5), custom_call_target="tpu_custom_call" | custom-call | flops 1912602624 | bytes 3325952 | tf_op jit(solution)/shard_map/pallas_call | solution.py:329
  92.1 0.9 shard_map.94
